TPU v7x, 32 devices: a whole 2x2x4 slice. The times are simulated.
32 devices in a mesh: radial: 8 (over y, x, core), axial: 4 (over z).
Axes of the slice: x: 2, y: 2, z: 4, core: 2. Of those that a mesh axis runs over, the one named last changes fastest.
Arguments:
- rhs: float32 [2, 2, 96, 64, 512], P(None, None, None, 'radial', 'axial'), may hold values from -6 to 6
- mat_ids: int32 [96, 64, 512], P(None, 'radial', 'axial'), may hold values from 0 to 3
- stiff_table: float32 [4], replicated, may hold values from 0.5 to 4
- dens_table: float32 [4], replicated, may hold values from 0.5 to 2
- mass_shift: float32 [2], replicated, may hold values from 0.5 to 2
- harmonic: int32 [2], replicated, may hold values from 1 to 12
- radial_factor: float32 [2, 2, 16, 16], replicated, may hold values from -0.09375 to 0.09375
- axial_factor: float32 [2, 2, 64, 64], replicated, may hold values from -0.046875 to 0.046875
Outputs:
- solution: float32 [2, 2, 96, 64, 512], P(None, None, None, 'radial', 'axial')
- residual: float32 [2, 2, 96, 64, 512], P(None, None, None, 'radial', 'axial')
All inputs are finite; a program needn't handle non-finite values.
Results may differ from a plain program's by a relative error of at most 0.00021.
Values sent between devices are 32-bit elements; how exact they have to be, the bound alone decides.
A program may use at most 128 MiB of HBM per device.

v0:
```python
import functools

import jax
import jax.numpy as jnp
from jax import lax
from jax.experimental import pallas as pl
from jax.experimental.pallas import tpu as pltpu
from jax.sharding import PartitionSpec as P

ITERS = 3
NSECT = 24
AR = 4
AA = 8
LOSS_FACTOR = 0.2
RELAXATION = 0.6
MESH = pl.DeviceIdType.MESH
HIGHEST = lax.Precision.HIGHEST
CHUNK = 8


def kernel(
    nrad,
    nax,
    rhs_hbm,
    ids_hbm,
    stiff_hbm,
    dens_hbm,
    mass_hbm,
    harm_hbm,
    radial_hbm,
    axial_hbm,
    sol_ref,
    res_ref,
    rhs_ref,
    ids_ref,
    stiff_ref,
    dens_ref,
    mass_ref,
    harm_ref,
    radial_ref,
    axial_ref,
    in_sem,
    stiff,
    wr_up,
    wr_dn,
    wa_lo,
    wa_hi,
    wt,
    dr,
    di,
    sc,
    srow_s,
    srow_r,
    scol_s,
    scol_r,
    row_s,
    row_r,
    col_s,
    col_r,
    col_m,
    one_s,
    one_r,
    two_r,
    axmat,
    radmat,
    st_send,
    st_recv,
    ha_send,
    ha_recv,
    g1_send,
    g1_recv,
    g2_send,
    g2_recv,
):
    loads = [
        pltpu.make_async_copy(src, dst, in_sem.at[n])
        for n, (src, dst) in enumerate(
            (
                (stiff_hbm, stiff_ref),
                (ids_hbm, ids_ref),
                (rhs_hbm, rhs_ref),
                (dens_hbm, dens_ref),
                (mass_hbm, mass_ref),
                (harm_hbm, harm_ref),
                (radial_hbm, radial_ref),
                (axial_hbm, axial_ref),
            )
        )
    ]
    for load_in in loads:
        load_in.start()
    ct = rhs_ref.shape[2]
    rows, lanes = rhs_ref.shape[3:]
    gr = radial_ref.shape[2]
    ga = axial_ref.shape[2]
    band_r = rows // AR
    band_c = lanes // AA
    i = lax.axis_index("radial")
    j = lax.axis_index("axial")
    has_up, has_dn = i > 0, i < nrad - 1
    has_lo, has_hi = j > 0, j < nax - 1
    conds = (has_up, has_dn, has_lo, has_hi)
    targets = ({"radial": i - 1}, {"radial": i + 1}, {"axial": j - 1}, {"axial": j + 1})

    for d in range(4):

        @pl.when(jnp.logical_not(conds[d]))
        def _():
            if d < 2:
                srow_r[d] = jnp.zeros(srow_r.shape[1:], jnp.float32)
                for k in range(ITERS):
                    row_r[k, d] = jnp.zeros(row_r.shape[2:], jnp.float32)
            else:
                scol_r[d - 2] = jnp.zeros(scol_r.shape[1:], jnp.float32)
                for k in range(ITERS):
                    col_r[k, d - 2] = jnp.zeros(col_r.shape[2:], jnp.float32)

    barrier = pltpu.get_barrier_semaphore()
    for d in range(1, nax):
        pl.semaphore_signal(
            barrier, inc=1, device_id={"axial": lax.rem(j + d, nax)}, device_id_type=MESH
        )
    for d in range(1, nrad):
        pl.semaphore_signal(
            barrier, inc=1, device_id={"radial": lax.rem(i + d, nrad)}, device_id_type=MESH
        )

    row = lax.broadcasted_iota(jnp.int32, (rows, lanes), 0)
    lane = lax.broadcasted_iota(jnp.int32, (rows, lanes), 1)
    zero = jnp.zeros((rows, lanes), jnp.float32)

    def lookup(ids, table):
        value = jnp.full(ids.shape, table[0], jnp.float32)
        for entry in range(1, table.shape[0]):
            value = jnp.where(ids == entry, table[entry], value)
        return value

    cap = lanes // 2
    pair = lane // 2

    def pack(value, t, packed):
        at = lax.rem(t, cap)
        return jnp.where(pair == at, pltpu.roll(value, 2 * at + 1, 1), packed)

    def stiff_copy(d):
        if d < 2:
            src, dst = srow_s.at[d], srow_r.at[1 - d]
        else:
            src, dst = scol_s, scol_r.at[3 - d]
        return pltpu.make_async_remote_copy(
            src_ref=src,
            dst_ref=dst,
            send_sem=st_send.at[d],
            recv_sem=st_recv.at[d ^ 1],
            device_id=targets[d],
            device_id_type=MESH,
        )

    middle = 3 * (ct // CHUNK) // 4

    def halo_copy(k, d, late=1):
        if d < 2:
            part = pl.ds(middle * CHUNK, ct - middle * CHUNK) if late else pl.ds(0, middle * CHUNK)
            src, dst = row_s.at[k, d, :, part], row_r.at[k, 1 - d, :, part]
        else:
            src, dst = col_s.at[k], col_r.at[k, 3 - d]
        return pltpu.make_async_remote_copy(
            src_ref=src,
            dst_ref=dst,
            send_sem=ha_send.at[k, late, d],
            recv_sem=ha_recv.at[k, late, d ^ 1],
            device_id=targets[d],
            device_id_type=MESH,
        )

    def gather_one(k, d):
        return pltpu.make_async_remote_copy(
            src_ref=one_s.at[k],
            dst_ref=one_r.at[k, j],
            send_sem=g1_send.at[k, d],
            recv_sem=g1_recv.at[k, d],
            device_id={"axial": lax.rem(j + d, nax)},
            device_id_type=MESH,
        )

    def gather_two(k, d):
        return pltpu.make_async_remote_copy(
            src_ref=two_r.at[k, i],
            dst_ref=two_r.at[k, i],
            send_sem=g2_send.at[k, d],
            recv_sem=g2_recv.at[k, d],
            device_id={"radial": lax.rem(i + d, nrad)},
            device_id_type=MESH,
        )

    def on_faces(act, faces=4):
        for d in range(faces):

            @pl.when(conds[d])
            def _():
                act(d)

    scol_s[...] = jnp.zeros(scol_s.shape, jnp.float32)
    col_s[...] = jnp.zeros(col_s.shape, jnp.float32)
    loads[0].wait()
    loads[1].wait()

    @pl.loop(0, ct // CHUNK)
    def _(chunk):
        begin = chunk * CHUNK
        tile = begin // cap
        packed = scol_s[tile]
        for u in range(CHUNK):
            t = begin + u
            value = lookup(ids_ref[t], stiff_ref)
            stiff[t + 1] = value
            srow_s[0, pl.ds(t, 1), :] = value[0:1]
            srow_s[1, pl.ds(t, 1), :] = value[rows - 1 : rows]
            packed = pack(value, t, packed)
        scol_s[tile] = packed

    stiff[0] = stiff[ct]
    stiff[ct + 1] = stiff[1]

    pl.semaphore_wait(barrier, nax + nrad - 2)
    on_faces(lambda d: stiff_copy(d).start())

    e_row = lax.broadcasted_iota(jnp.int32, (lanes, lanes), 0)
    e_col = lax.broadcasted_iota(jnp.int32, (lanes, lanes), 1)
    fold = jnp.where(e_row // AA + j * band_c == e_col, 1.0, 0.0)

    def restrict_and_send(k, sums):
        tile = zero
        for c in range(4):
            s = sums[c] + pltpu.roll(sums[c], rows - 1, 0)
            s = s + pltpu.roll(s, rows - 2, 0)
            for g in range(band_r):
                to = c * band_r + g
                moved = pltpu.roll(s, (to - g * AR) % rows, 0)
                tile = jnp.where(row == to, moved, tile)
        one_s[k] = jnp.dot(tile, fold, precision=HIGHEST, preferred_element_type=jnp.float32)
        for d in range(1, nax):
            gather_one(k, d).start()

    loads[2].wait()

    def sum_pass(chunk, sums):
        sums = list(sums)
        for u in range(CHUNK):
            for c in range(4):
                sums[c] = sums[c] + rhs_ref[c // 2, c % 2, chunk * CHUNK + u]
        return tuple(sums)

    restrict_and_send(0, lax.fori_loop(0, ct // CHUNK, sum_pass, (zero,) * 4))
    for load_in in loads[3:]:
        load_in.wait()

    ax_row = lax.broadcasted_iota(jnp.int32, (lanes, ga), 0)
    ax_col = lax.broadcasted_iota(jnp.int32, (lanes, ga), 1)
    own = jnp.where(ax_row // AA + j * band_c == ax_col, 1.0, 0.0)
    edge_lo = j * band_c - 1
    edge_hi = (j + 1) * band_c
    half = lanes // 2
    edges = []
    for p in range(2):
        hit = ((ax_row == p * half) & (ax_col == edge_lo)) | (
            (ax_row == p * half + 1) & (ax_col == edge_hi)
        )
        edges.append(jnp.where(hit, 1.0, 0.0))
    for h in range(2):
        if ga < lanes:
            axmat[h] = jnp.zeros(axmat.shape[1:], jnp.float32)

        def spread(select, p):
            return jnp.dot(
                select, axial_ref[p, h], precision=HIGHEST, preferred_element_type=jnp.float32
            )

        axmat[h, 0:lanes, 0:ga] = spread(own, 0)
        axmat[h, lanes : 2 * lanes, 0:ga] = spread(own, 1)
        axmat[h, 2 * lanes : 3 * lanes, 0:ga] = spread(edges[0], 0) + spread(edges[1], 1)

    per = 2 * rows
    cdev = 4 * band_r
    r_row = lax.broadcasted_iota(jnp.int32, (4 * per, gr), 0) % per
    r_col = lax.broadcasted_iota(jnp.int32, (4 * per, gr), 1)
    want = jnp.where(
        r_row < rows,
        r_row // AR + i * band_r,
        jnp.where(
            r_row == rows, i * band_r - 1, jnp.where(r_row == rows + 1, (i + 1) * band_r, -1)
        ),
    )
    r_sel = jnp.where(want == r_col, 1.0, 0.0)
    c_row = lax.broadcasted_iota(jnp.int32, (gr, nrad * cdev), 0)
    c_col = lax.broadcasted_iota(jnp.int32, (gr, nrad * cdev), 1)
    c_sel = jnp.where((c_col // cdev) * band_r + c_col % band_r == c_row, 1.0, 0.0)
    m_out = lax.broadcasted_iota(jnp.int32, (4 * per, nrad * cdev), 0) // per
    m_in = (lax.broadcasted_iota(jnp.int32, (4 * per, nrad * cdev), 1) % cdev) // band_r
    built = jnp.zeros((4 * per, nrad * cdev), jnp.float32)
    for h in range(2):
        for p in range(2):
            part = jnp.dot(
                jnp.dot(
                    r_sel, radial_ref[p, h], precision=HIGHEST, preferred_element_type=jnp.float32
                ),
                c_sel,
                precision=HIGHEST,
                preferred_element_type=jnp.float32,
            )
            if p == 0:
                built = jnp.where((m_out == m_in) & (m_out % 2 == h), part, built)
            else:
                built = jnp.where((m_out == h) & (m_in == 2 + h), -part, built)
                built = jnp.where((m_out == 2 + h) & (m_in == h), part, built)
    radmat[...] = built

    def mix_and_send(k):
        total = one_s[k]
        for d in range(1, nax):
            gather_one(k, d).wait_recv()
        for d in range(1, nax):
            total = total + one_r[k, lax.rem(j + d, nax)]
        outs = []
        for h in range(2):
            prod = lax.dot_general(
                total,
                axmat[h],
                (((1,), (1,)), ((), ())),
                precision=HIGHEST,
                preferred_element_type=jnp.float32,
            )
            a = prod[:, 0:lanes]
            b = prod[:, lanes : 2 * lanes]
            e = prod[:, 2 * lanes : 3 * lanes]
            f = pltpu.roll(e, half, 1)
            swap_b = pltpu.roll(b, rows // 2, 0)
            swap_f = pltpu.roll(f, rows // 2, 0)
            low = row < rows // 2
            outs.append(
                (jnp.where(low, a - swap_b, a + swap_b), jnp.where(low, e - swap_f, e + swap_f))
            )
        odd = (row // band_r) % 2 == 1
        two_r[k, i, :, 0:lanes] = jnp.where(odd, outs[1][0], outs[0][0])
        two_r[k, i, :, lanes : 2 * lanes] = jnp.where(odd, outs[1][1], outs[0][1])
        for d in range(1, nrad):
            gather_two(k, d).start()

    def finish_coarse(k):
        for d in range(1, nrad):
            gather_two(k, d).wait_recv()
        return jnp.dot(
            radmat[...],
            two_r[k].reshape(nrad * cdev, 2 * lanes),
            precision=HIGHEST,
            preferred_element_type=jnp.float32,
        )

    mix_and_send(0)
    on_faces(lambda d: stiff_copy(d ^ 1).wait_recv())

    mass = [mass_ref[0], mass_ref[1]]

    odd_lane = lane % 2 == 1

    def around(value, up, dn, beside, t):
        edge = pltpu.roll(beside, lanes - 1 - 2 * lax.rem(t, cap), 1)
        return (
            jnp.where(row == 0, up, pltpu.roll(value, 1, 0)),
            jnp.where(row == rows - 1, dn, pltpu.roll(value, rows - 1, 0)),
            pltpu.roll(jnp.where(lane == lanes - 1, edge, value), 1, 1),
            pltpu.roll(jnp.where(lane == 0, edge, value), lanes - 1, 1),
        )

    def put_rows(k, t, y):
        for c in range(4):
            row_s[k, 0, c, pl.ds(t, 1), :] = y[c][0:1]
            row_s[k, 1, c, pl.ds(t, 1), :] = y[c][rows - 1 : rows]

    def smooth(t, rr, ri, h):
        d_re, d_im, scale = dr[h, t], di[t], sc[h, t]
        return (d_re * rr + d_im * ri) * scale, (d_re * ri - d_im * rr) * scale

    for n in range(scol_s.shape[0]):
        col_m[0, n] = jnp.where(odd_lane, scol_r[1, n], scol_r[0, n])

    def setup_step(t, packs, beside):
        value = stiff[t + 1]
        up, dn, lo, hi = around(
            value,
            srow_r[0, pl.ds(t, 1), :],
            srow_r[1, pl.ds(t, 1), :],
            beside,
            t,
        )
        c_up, c_dn = 0.5 * (value + up), 0.5 * (value + dn)
        c_lo, c_hi = 0.5 * (value + lo), 0.5 * (value + hi)
        c_be, c_ah = 0.5 * (value + stiff[t]), 0.5 * (value + stiff[t + 2])
        wr_up[t] = c_up
        wr_dn[t] = c_dn
        wa_lo[t] = c_lo
        wa_hi[t] = c_hi
        wt[t] = c_be
        wt[t + 1] = c_ah
        total = c_dn + c_up + c_hi + c_lo + c_ah + c_be
        density = lookup(ids_ref[t], dens_ref)
        d_im = LOSS_FACTOR * total
        di[t] = d_im
        y = [None] * 4
        for h in range(2):
            d_re = total - mass[h] * density
            scale = RELAXATION / (d_re * d_re + d_im * d_im)
            dr[h, t] = d_re
            sc[h, t] = scale
            rr, ri = rhs_ref[0, h, t], rhs_ref[1, h, t]
            y[h] = (d_re * rr + d_im * ri) * scale
            y[2 + h] = (d_re * ri - d_im * rr) * scale
            sol_ref[0, h, t] = y[h]
            sol_ref[1, h, t] = y[2 + h]
        put_rows(0, t, y)
        return [pack(y[c], t, packs[c]) for c in range(4)]

    def setup_chunk(chunk, nothing):
        begin = chunk * CHUNK
        tile = begin // cap
        beside = col_m[0, tile]
        packs = [col_s[0, c, tile] for c in range(4)]
        for u in range(CHUNK):
            packs = setup_step(begin + u, packs, beside)
        for c in range(4):
            col_s[0, c, tile] = packs[c]
        return nothing

    lax.fori_loop(0, middle, setup_chunk, 0)
    on_faces(lambda d: halo_copy(0, d, 0).start(), 2)
    lax.fori_loop(middle, ct // CHUNK, setup_chunk, 0)
    on_faces(lambda d: halo_copy(0, d).start())

    cosines, sines = [], []
    for h in range(2):
        angle = jnp.full((rows, lanes), harm_ref[h], jnp.int32).astype(jnp.float32) * (
            2.0 * jnp.pi / NSECT
        )
        cosines.append(jnp.cos(angle))
        sines.append(jnp.sin(angle))

    for k in range(ITERS):
        final = k == ITERS - 1
        coarse = finish_coarse(k)
        corr = [coarse[c * per : c * per + rows, 0:lanes] for c in range(4)]
        on_faces(lambda d: halo_copy(k, d ^ 1, 0).wait_recv(), 2)
        on_faces(lambda d: halo_copy(k, d ^ 1).wait_recv())
        for c in range(4):
            add = []
            for side in range(2):
                at = c * per + rows + side
                row_r[k, side, c] = row_r[k, side, c] + coarse[at : at + 1, 0:lanes]
                add.append(coarse[c * per : c * per + rows, lanes + side : lanes + side + 1])
            for n in range(col_m.shape[1]):
                col_m[c, n] = jnp.where(
                    odd_lane, col_r[k, 1, c, n] + add[1], col_r[k, 0, c, n] + add[0]
                )

        def load(t):
            return [sol_ref[c // 2, c % 2, t] + corr[c] for c in range(4)]

        def turn(x, sign):
            return [cosines[h] * x[h] - sign * sines[h] * x[2 + h] for h in range(2)] + [
                sign * sines[h] * x[h] + cosines[h] * x[2 + h] for h in range(2)
            ]

        start = load(0)
        beyond = turn(start, 1.0)
        before = turn(load(ct - 1), -1.0)

        def stencil(t, xm, x, xp, beside):
            c_up, c_dn, c_lo, c_hi = wr_up[t], wr_dn[t], wa_lo[t], wa_hi[t]
            c_be, c_ah = wt[t], wt[t + 1]
            nb = []
            for c in range(4):
                up, dn, lo, hi = around(
                    x[c],
                    row_r[k, 0, c, pl.ds(t, 1), :],
                    row_r[k, 1, c, pl.ds(t, 1), :],
                    beside[c],
                    t,
                )
                nb.append(
                    (c_dn * dn + c_up * up)
                    + (c_hi * hi + c_lo * lo)
                    + (c_ah * xp[c] + c_be * xm[c])
                )
            d_im = di[t]
            res = [None] * 4
            for h in range(2):
                d_re = dr[h, t]
                re, im = h, 2 + h
                res[re] = rhs_ref[0, h, t] - (
                    d_re * x[re] - d_im * x[im] - (nb[re] - LOSS_FACTOR * nb[im])
                )
                res[im] = rhs_ref[1, h, t] - (
                    d_re * x[im] + d_im * x[re] - (nb[im] + LOSS_FACTOR * nb[re])
                )
            return res

        def chunk_pass(chunk, carry):
            xm, x, sums = list(carry[0:4]), list(carry[4:8]), list(carry[8:])
            begin = chunk * CHUNK
            tile = begin // cap
            beside = [col_m[c, tile] for c in range(4)]
            if not final:
                packs = [col_s[k + 1, c, tile] for c in range(4)]
            for u in range(CHUNK):
                t = begin + u
                if u < CHUNK - 1:
                    xp = load(t + 1)
                else:
                    ended = t == ct - 1
                    xp = load(jnp.minimum(t + 1, ct - 1))
                    xp = [jnp.where(ended, beyond[c], xp[c]) for c in range(4)]
                res = stencil(t, xm, x, xp, beside)
                if final:
                    for c in range(4):
                        sol_ref[c // 2, c % 2, t] = x[c]
                        res_ref[c // 2, c % 2, t] = res[c]
                else:
                    y = [None] * 4
                    for h in range(2):
                        a, b = smooth(t, res[h], res[2 + h], h)
                        y[h], y[2 + h] = x[h] + a, x[2 + h] + b
                    for c in range(4):
                        sol_ref[c // 2, c % 2, t] = y[c]
                        sums[c] = sums[c] + res[c]
                        packs[c] = pack(y[c], t, packs[c])
                    put_rows(k + 1, t, y)
                xm, x = x, xp
            if not final:
                for c in range(4):
                    col_s[k + 1, c, tile] = packs[c]
            return tuple(xm) + tuple(x) + tuple(sums)

        state = () if final else (zero,) * 4
        carry = tuple(before) + tuple(start) + state
        if final:
            lax.fori_loop(0, ct // CHUNK, chunk_pass, carry)
        else:
            carry = lax.fori_loop(0, middle, chunk_pass, carry)
            on_faces(lambda d: halo_copy(k + 1, d, 0).start(), 2)
            carry = lax.fori_loop(middle, ct // CHUNK, chunk_pass, carry)
        if not final:
            restrict_and_send(k + 1, carry[8:])
            on_faces(lambda d: halo_copy(k + 1, d).start())
            mix_and_send(k + 1)

    on_faces(lambda d: stiff_copy(d).wait_send())
    for k in range(ITERS):
        on_faces(lambda d: halo_copy(k, d, 0).wait_send(), 2)
        on_faces(lambda d: halo_copy(k, d).wait_send())
        for d in range(1, nax):
            gather_one(k, d).wait_send()
        for d in range(1, nrad):
            gather_two(k, d).wait_send()


def local(rhs, mat_ids, stiff_table, dens_table, mass_shift, harmonic, radial_factor, axial_factor):
    nrad = lax.axis_size("radial")
    nax = lax.axis_size("axial")
    ct, rows, lanes = mat_ids.shape
    vmem = pl.BlockSpec(memory_space=pltpu.VMEM)
    hbm = pl.BlockSpec(memory_space=pltpu.HBM)
    tiles = -(-2 * ct // lanes)
    f32 = jnp.float32
    field = (ct, rows, lanes)
    cdev = 4 * (rows // AR)
    dma = pltpu.SemaphoreType.DMA
    return pl.pallas_call(
        functools.partial(kernel, nrad, nax),
        out_shape=(jax.ShapeDtypeStruct(rhs.shape, f32), jax.ShapeDtypeStruct(rhs.shape, f32)),
        in_specs=[hbm] * 8,
        out_specs=(vmem, vmem),
        scratch_shapes=[
            pltpu.VMEM(rhs.shape, f32),
            pltpu.VMEM(field, jnp.int32),
            pltpu.SMEM(stiff_table.shape, f32),
            pltpu.SMEM(dens_table.shape, f32),
            pltpu.SMEM(mass_shift.shape, f32),
            pltpu.SMEM(harmonic.shape, jnp.int32),
            pltpu.VMEM(radial_factor.shape, f32),
            pltpu.VMEM(axial_factor.shape, f32),
            dma((8,)),
            pltpu.VMEM((ct + 2, rows, lanes), f32),
            pltpu.VMEM(field, f32),
            pltpu.VMEM(field, f32),
            pltpu.VMEM(field, f32),
            pltpu.VMEM(field, f32),
            pltpu.VMEM((ct + 1, rows, lanes), f32),
            pltpu.VMEM((2,) + field, f32),
            pltpu.VMEM(field, f32),
            pltpu.VMEM((2,) + field, f32),
            pltpu.VMEM((2, ct, lanes), f32),
            pltpu.VMEM((2, ct, lanes), f32),
            pltpu.VMEM((tiles, rows, lanes), f32),
            pltpu.VMEM((2, tiles, rows, lanes), f32),
            pltpu.VMEM((ITERS, 2, 4, ct, lanes), f32),
            pltpu.VMEM((ITERS, 2, 4, ct, lanes), f32),
            pltpu.VMEM((ITERS, 4, tiles, rows, lanes), f32),
            pltpu.VMEM((ITERS, 2, 4, tiles, rows, lanes), f32),
            pltpu.VMEM((4, tiles, rows, lanes), f32),
            pltpu.VMEM((ITERS, rows, lanes), f32),
            pltpu.VMEM((ITERS, nax, rows, lanes), f32),
            pltpu.VMEM((ITERS, nrad, rows, 2 * lanes), f32),
            pltpu.VMEM((2, 3 * lanes, lanes), f32),
            pltpu.VMEM((8 * rows, nrad * cdev), f32),
            dma((4,)),
            dma((4,)),
            dma((ITERS, 2, 4)),
            dma((ITERS, 2, 4)),
            dma((ITERS, nax)),
            dma((ITERS, nax)),
            dma((ITERS, nrad)),
            dma((ITERS, nrad)),
        ],
        compiler_params=pltpu.CompilerParams(
            collective_id=0, has_side_effects=True, vmem_limit_bytes=58 * 1024 * 1024
        ),
    )(rhs, mat_ids, stiff_table, dens_table, mass_shift, harmonic, radial_factor, axial_factor)


def solution(mesh):
    return jax.shard_map(
        local,
        mesh=mesh,
        in_specs=(
            P(None, None, None, "radial", "axial"),
            P(None, "radial", "axial"),
            P(),
            P(),
            P(),
            P(),
            P(),
            P(),
        ),
        out_specs=(P(None, None, None, "radial", "axial"), P(None, None, None, "radial", "axial")),
        check_vma=False,
    )
```

profile of v0, /device:TPU:1, one launch (start us, length us, event | category | flops | bytes accessed | tf_op | source)
XLA Modules:
  0.0 49.6 jit_solution(12599899695085496818)
XLA Ops:
  0.6 45.0 %shard_map.95 = (f32[2,2,96,8,128]{4,3,2,1,0:T(8,128)}, f32[2,2,96,8,128]{4,3,2,1,0:T(8,128)}) custom-call(f32[2,2,96,8,128]{4,3,2,1,0:T(8,128)} %rhs_hbm.1, s32[96,8,128]{2,1,0:T(8,128)} %ids_hbm.1, f32[4]{0:T(128)} %stiff_hbm.1, f32[4]{0:T(128)} %dens_hbm.1, f32[2]{0:T(128)} %mass_hbm.1, s32[2]{0:T(128)} %harm_hbm.1, f32[2,2,16,16]{3,2,1,0:T(8,128)} %radial_hbm.1, ...), custom_call_target="tpu_custom_call" | custom-call | tf_op jit(solution)/shard_map/pallas_call | solution.py:576
  45.6 0.0 copy-start
  45.7 2.8 %copy.12 = f32[2,2,96,8,128]{4,3,2,1,0:T(8,128)} copy(f32[2,2,96,8,128]{4,3,2,1,0:T(8,128)} %get-tuple-element.4) | data formatting | bytes 3145728
  48.4 0.0 copy-done
  48.4 1.1 %copy.13 = f32[2,2,96,8,128]{4,3,2,1,0:T(8,128)} copy(f32[2,2,96,8,128]{4,3,2,1,0:T(8,128)S(1)} %copy-done) | data formatting | bytes 3145728
Async XLA Ops:
  45.6 2.8 %copy-start = (f32[2,2,96,8,128]{4,3,2,1,0:T(8,128)S(1)}, f32[2,2,96,8,128]{4,3,2,1,0:T(8,128)}, u32[]{:S(2)}) copy-start(f32[2,2,96,8,128]{4,3,2,1,0:T(8,128)} %get-tuple-element.5) | copy-start | bytes 4718596
where the time goes:
time: 50.1 us; the launch traced here: 49.6 us
  Pallas kernels  45 us (90%)
  local copies, waits for them, and re-layouts  3.92 us (8%)
  between operations  0.65 us (1%)
    pallas_call x1, Pallas kernels, local(): pl.pallas_call(functools.partial(kernel, nrad, nax), out_shape=(jax.Shape...  45 us
    unnamed x4, local copies, waits for them, and re-layouts  3.92 us

commit v1 on v0

--- a/solution.py
+++ b/solution.py
@@ -573,9 +573,9 @@
     field = (ct, rows, lanes)
     cdev = 4 * (rows // AR)
     dma = pltpu.SemaphoreType.DMA
-    return pl.pallas_call(
+    sol, res = pl.pallas_call(
         functools.partial(kernel, nrad, nax),
-        out_shape=(jax.ShapeDtypeStruct(rhs.shape, f32), jax.ShapeDtypeStruct(rhs.shape, f32)),
+        out_shape=(pltpu.VMEM(rhs.shape, f32), pltpu.VMEM(rhs.shape, f32)),
         in_specs=[hbm] * 8,
         out_specs=(vmem, vmem),
         scratch_shapes=[
@@ -621,9 +621,27 @@
             dma((ITERS, nrad)),
         ],
         compiler_params=pltpu.CompilerParams(
-            collective_id=0, has_side_effects=True, vmem_limit_bytes=58 * 1024 * 1024
+            collective_id=0, has_side_effects=True, vmem_limit_bytes=40 * 1024 * 1024
         ),
-    )(rhs, mat_ids, stiff_table, dens_table, mass_shift, harmonic, radial_factor, axial_factor)
+    )(*[pltpu.with_memory_space_constraint(x, pltpu.HBM) for x in (rhs, mat_ids, stiff_table, dens_table, mass_shift, harmonic, radial_factor, axial_factor)])
+    return pl.pallas_call(
+        put_out,
+        out_shape=(jax.ShapeDtypeStruct(rhs.shape, f32), jax.ShapeDtypeStruct(rhs.shape, f32)),
+        in_specs=[vmem] * 2,
+        out_specs=(hbm, hbm),
+        scratch_shapes=[dma((2, 4))],
+    )(pltpu.with_memory_space_constraint(sol, pltpu.VMEM), pltpu.with_memory_space_constraint(res, pltpu.VMEM))
+
+
+def put_out(a_ref, b_ref, x_ref, y_ref, sem):
+    copies = []
+    for n, (src, dst) in enumerate(((a_ref, x_ref), (b_ref, y_ref))):
+        for c in range(4):
+            copies.append(pltpu.make_async_copy(src.at[c // 2, c % 2], dst.at[c // 2, c % 2], sem.at[n, c]))
+    for c in copies:
+        c.start()
+    for c in copies:
+        c.wait()
 
 
 def solution(mesh):

time: 50.1 us -> 46.2 us (0.922)
  local copies, waits for them, and re-layouts: 3.92 us -> 0 us
    unnamed x4 -> x0, local copies, waits for them, and re-layouts: 3.92 us -> none
    pallas_call x1 -> x2, Pallas kernels: 45 us -> 45.1 us  [the longest x1 43.3 us: local(): pl.pallas_call(functools.partial(kernel, nrad, nax), out_shape=(pltpu.VME...]
where the time goes in v1:
time: 46.2 us; the launch traced here: 45.7 us
  Pallas kernels  45.1 us (98%)
  between operations  0.64 us (1%)
    pallas_call x1, Pallas kernels, local(): pl.pallas_call(functools.partial(kernel, nrad, nax), out_shape=(pltpu.VME...  43.3 us
    pallas_call x1, Pallas kernels, local(): pl.pallas_call(put_out, out_shape=(jax.ShapeDtypeStruct(rhs.shape, f32),...  1.72 us

profile of v1, /device:TPU:1, one launch (start us, length us, event | category | flops | bytes accessed | tf_op | source)
XLA Modules:
  0.0 45.7 jit_solution(1893674898626985840)
XLA Ops:
  0.6 43.3 %shard_map.95 = (f32[2,2,96,8,128]{4,3,2,1,0:T(8,128)S(1)}, f32[2,2,96,8,128]{4,3,2,1,0:T(8,128)S(1)}) custom-call(f32[2,2,96,8,128]{4,3,2,1,0:T(8,128)} %rhs_hbm.1, s32[96,8,128]{2,1,0:T(8,128)} %ids_hbm.1, f32[4]{0:T(128)} %stiff_hbm.1, f32[4]{0:T(128)} %dens_hbm.1, f32[2]{0:T(128)} %mass_hbm.1, s32[2]{0:T(128)} %harm_hbm.1, f32[2,2,16,16]{3,2,1,0:T(8,128)} %radial_hbm.1, ...), custom_call_target="tpu_custom_call" | custom-call | tf_op jit(solution)/shard_map/pallas_call | solution.py:576
  44.0 1.7 %shard_map.96 = (f32[2,2,96,8,128]{4,3,2,1,0:T(8,128)}, f32[2,2,96,8,128]{4,3,2,1,0:T(8,128)}) custom-call(f32[2,2,96,8,128]{4,3,2,1,0:T(8,128)S(1)} %get-tuple-element.4.a_ref, f32[2,2,96,8,128]{4,3,2,1,0:T(8,128)S(1)} %get-tuple-element.5.b_ref), custom_call_target="tpu_custom_call" | custom-call | tf_op jit(solution)/shard_map/pallas_call | solution.py:627

commit v2 on v0

v2 whole, which is shorter than its diff:
```python
import functools

import jax
import jax.numpy as jnp
from jax import lax
from jax.experimental import pallas as pl
from jax.experimental.pallas import tpu as pltpu
from jax.sharding import PartitionSpec as P

ITERS = 3
NSECT = 24
AR = 4
AA = 8
LOSS_FACTOR = 0.2
RELAXATION = 0.6
MESH = pl.DeviceIdType.MESH
HIGHEST = lax.Precision.HIGHEST
CHUNK = 8
PARTS = 4
GROUP = 32


def dot(a, b):
    return jnp.dot(a, b, precision=HIGHEST, preferred_element_type=jnp.float32)


def grid_of(rows, lanes):
    return (
        lax.broadcasted_iota(jnp.int32, (rows, lanes), 0),
        lax.broadcasted_iota(jnp.int32, (rows, lanes), 1),
    )


def around(value, up, dn, edge):
    rows, lanes = value.shape
    row, lane = grid_of(rows, lanes)
    return (
        jnp.where(row == 0, up, pltpu.roll(value, 1, 0)),
        jnp.where(row == rows - 1, dn, pltpu.roll(value, rows - 1, 0)),
        pltpu.roll(jnp.where(lane == lanes - 1, edge, value), 1, 1),
        pltpu.roll(jnp.where(lane == 0, edge, value), lanes - 1, 1),
    )


def lossy(x):
    return [x[h] - LOSS_FACTOR * x[2 + h] for h in range(2)] + [
        x[2 + h] + LOSS_FACTOR * x[h] for h in range(2)
    ]


def coarse_change(weights, push, c):
    w_up, w_dn, w_lo, w_hi, dens = weights
    return ((w_up * push[0][c] + w_dn * push[1][c]) + (w_lo * push[2][c] + w_hi * push[3][c])) - (
        dens * push[4][c]
    )


def turn(trig, x, sign):
    cosines, sines = trig[0:2], trig[2:4]
    return [cosines[h] * x[h] - sign * sines[h] * x[2 + h] for h in range(2)] + [
        sign * sines[h] * x[h] + cosines[h] * x[2 + h] for h in range(2)
    ]


def kernel(
    nrad,
    nax,
    rhs_hbm,
    ids_hbm,
    stiff_hbm,
    dens_hbm,
    mass_hbm,
    harm_hbm,
    radial_hbm,
    axial_hbm,
    sol_ref,
    val_ref,
    wr_up,
    wr_dn,
    wa_lo,
    wa_hi,
    dens,
    corr_ref,
    push_ref,
    rhs_ref,
    ids_ref,
    stiff_ref,
    dens_ref,
    mass_ref,
    harm_ref,
    radial_ref,
    axial_ref,
    in_sem,
    stiff,
    wt,
    dr,
    di,
    sc,
    edge_ref,
    srow_s,
    srow_r,
    scol_s,
    scol_r,
    scol_m,
    row_r,
    col_s,
    col_r,
    all_r,
    axmat,
    radmat,
    st_send,
    st_recv,
    ha_send,
    ha_recv,
    ga_send,
    ga_recv,
):
    loads = [
        pltpu.make_async_copy(src, dst, in_sem.at[n])
        for n, (src, dst) in enumerate(
            (
                (stiff_hbm, stiff_ref),
                (ids_hbm, ids_ref),
                (rhs_hbm, rhs_ref),
                (dens_hbm, dens_ref),
                (mass_hbm, mass_ref),
                (harm_hbm, harm_ref),
                (radial_hbm, radial_ref),
                (axial_hbm, axial_ref),
            )
        )
    ]
    for load_in in loads:
        load_in.start()
    ct = rhs_ref.shape[2]
    rows, lanes = rhs_ref.shape[3:]
    gr = radial_ref.shape[2]
    ga = axial_ref.shape[2]
    band_r = rows // AR
    band_c = lanes // AA
    chunks = ct // CHUNK
    ndev = nrad * nax
    i = lax.axis_index("radial")
    j = lax.axis_index("axial")
    me = i * nax + j
    has_up, has_dn = i > 0, i < nrad - 1
    has_lo, has_hi = j > 0, j < nax - 1
    conds = (has_up, has_dn, has_lo, has_hi)
    targets = ({"radial": i - 1}, {"radial": i + 1}, {"axial": j - 1}, {"axial": j + 1})

    def peer(d):
        at = lax.rem(me + d, ndev)
        return {"radial": at // nax, "axial": lax.rem(at, nax)}

    barrier = pltpu.get_barrier_semaphore()

    @pl.loop(1, ndev)
    def _(d):
        pl.semaphore_signal(barrier, inc=1, device_id=peer(d), device_id_type=MESH)

    for d in range(4):

        @pl.when(jnp.logical_not(conds[d]))
        def _():
            if d < 2:
                srow_r[d] = jnp.zeros(srow_r.shape[1:], jnp.float32)
                for k in range(ITERS):
                    row_r[k, d] = jnp.zeros(row_r.shape[2:], jnp.float32)
            else:
                scol_r[d - 2] = jnp.zeros(scol_r.shape[1:], jnp.float32)
                for k in range(ITERS):
                    col_r[k, d - 2] = jnp.zeros(col_r.shape[2:], jnp.float32)

    row, lane = grid_of(rows, lanes)
    zero = jnp.zeros((rows, lanes), jnp.float32)
    pair = lane // 2
    odd_lane = lane % 2 == 1

    def lookup(ids, table):
        value = jnp.full(ids.shape, table[0], jnp.float32)
        for entry in range(1, table.shape[0]):
            value = jnp.where(ids == entry, table[entry], value)
        return value

    def pack(value, at, packed):
        return jnp.where(pair == at, pltpu.roll(value, (2 * at + 1) % lanes, 1), packed)

    def stiff_copy(d):
        if d < 2:
            src, dst = srow_s.at[d], srow_r.at[1 - d]
        else:
            src, dst = scol_s, scol_r.at[3 - d]
        return pltpu.make_async_remote_copy(
            src_ref=src,
            dst_ref=dst,
            send_sem=st_send.at[d],
            recv_sem=st_recv.at[d ^ 1],
            device_id=targets[d],
            device_id_type=MESH,
        )

    part_chunks = chunks // PARTS
    part_ct = ct // PARTS

    def halo_copy(k, part, d):
        if d < 2:
            at = pl.ds(part * part_ct, part_ct)
            line = pl.ds(0 if d == 0 else rows - 1, 1)
            src, dst = sol_ref.at[:, :, at, line], row_r.at[k, 1 - d, :, :, at]
        else:
            at = pl.ds(part * part_chunks, part_chunks)
            src, dst = col_s.at[k, at], col_r.at[k, 3 - d, at]
        return pltpu.make_async_remote_copy(
            src_ref=src,
            dst_ref=dst,
            send_sem=ha_send.at[k, part, d],
            recv_sem=ha_recv.at[k, part, d ^ 1],
            device_id=targets[d],
            device_id_type=MESH,
        )

    def gather(k, d):
        return pltpu.make_async_remote_copy(
            src_ref=all_r.at[k, me],
            dst_ref=all_r.at[k, me],
            send_sem=ga_send.at[k, d],
            recv_sem=ga_recv.at[k, d],
            device_id=peer(d),
            device_id_type=MESH,
        )

    def on_faces(act):
        for d in range(4):

            @pl.when(conds[d])
            def _():
                act(d)

    loads[0].wait()
    loads[1].wait()

    @pl.loop(0, ct // GROUP)
    def _(group):
        packed = zero
        for u in range(GROUP):
            t = group * GROUP + u
            value = lookup(ids_ref[t], stiff_ref)
            stiff[t + 1] = value
            srow_s[0, pl.ds(t, 1), :] = value[0:1]
            srow_s[1, pl.ds(t, 1), :] = value[rows - 1 : rows]
            packed = pack(value, u, packed)
        scol_s[group] = packed

    stiff[0] = stiff[ct]
    stiff[ct + 1] = stiff[1]

    pl.semaphore_wait(barrier, ndev - 1)
    on_faces(lambda d: stiff_copy(d).start())

    e_row, e_col = grid_of(lanes, lanes)
    fold = jnp.where(e_row // AA == e_col % band_c, 1.0, 0.0)
    k_row, k_col = grid_of(4 * rows, lanes)
    keep = k_row // AR == (j + rows - k_col // band_c) % rows

    def restrict_and_send(k, sums):
        folded = dot(jnp.concatenate(sums, axis=0), fold)
        all_r[k, me] = jnp.sum(jnp.where(keep, folded, 0.0), axis=0, keepdims=True)

        @pl.loop(1, ndev)
        def _(d):
            gather(k, d).start()

    loads[2].wait()

    def sum_pass(chunk, sums):
        sums = list(sums)
        for u in range(CHUNK):
            for c in range(4):
                sums[c] = sums[c] + rhs_ref[c // 2, c % 2, chunk * CHUNK + u]
        return tuple(sums)

    restrict_and_send(0, lax.fori_loop(0, chunks, sum_pass, (zero,) * 4))
    for load_in in loads[3:]:
        load_in.wait()

    ax_row, ax_col = grid_of(lanes, ga)
    own = jnp.where(ax_row // AA + j * band_c == ax_col, 1.0, 0.0)
    half = lanes // 2
    side = jnp.where(ax_row % 2 == 0, j * band_c - 1, (j + 1) * band_c) == ax_col
    edges = [jnp.where(side & (ax_row // half == p), 1.0, 0.0) for p in range(2)]
    for h in range(2):
        if ga < lanes:
            axmat[h] = jnp.zeros(axmat.shape[1:], jnp.float32)
        axmat[h, 0:lanes, 0:ga] = dot(own, axial_ref[0, h])
        axmat[h, lanes : 2 * lanes, 0:ga] = dot(own, axial_ref[1, h])
        axmat[h, 2 * lanes : 3 * lanes, 0:ga] = dot(edges[0], axial_ref[0, h]) + dot(
            edges[1], axial_ref[1, h]
        )

    per = 2 * rows
    cdev = 4 * band_r
    r_row, r_col = grid_of(4 * per, gr)
    r_row = r_row % per
    want = jnp.where(
        r_row < rows,
        r_row // AR + i * band_r,
        jnp.where(
            r_row == rows, i * band_r - 1, jnp.where(r_row == rows + 1, (i + 1) * band_r, -1)
        ),
    )
    r_sel = jnp.where(want == r_col, 1.0, 0.0)
    c_row, c_col = grid_of(gr, nrad * cdev)
    c_sel = jnp.where((c_col // cdev) * band_r + c_col % band_r == c_row, 1.0, 0.0)
    m_row, m_col = grid_of(4 * per, nrad * cdev)
    m_out = m_row // per
    m_in = (m_col % cdev) // band_r
    first = jnp.zeros((4 * per, nrad * cdev), jnp.float32)
    second = first
    for h in range(2):
        same = (m_out == m_in) & (m_out % 2 == h)
        to_re = (m_out == h) & (m_in == 2 + h)
        to_im = (m_out == 2 + h) & (m_in == h)
        real = dot(dot(r_sel, radial_ref[0, h]), c_sel)
        imag = dot(dot(r_sel, radial_ref[1, h]), c_sel)
        first = jnp.where(same, real, first)
        first = jnp.where(to_re, -imag, first)
        first = jnp.where(to_im, imag, first)
        second = jnp.where(same, -imag, second)
        second = jnp.where(to_re, -real, second)
        second = jnp.where(to_im, real, second)
    radmat[:, 0 : nrad * cdev] = first
    radmat[:, nrad * cdev : 2 * nrad * cdev] = second

    p_row, _ = grid_of(nrad * cdev, 3 * lanes)
    odd_harm = (p_row // band_r) % 2 == 1

    def finish_coarse(k):
        @pl.loop(1, ndev)
        def _(d):
            gather(k, d).wait_recv()

        tiles = []
        for a in range(nrad):
            tile = zero
            for b in range(nax):
                tile = jnp.where((lane // band_c + row) % rows == b, all_r[k, a * nax + b], tile)
            tile = pltpu.roll(tile, 0, 1, stride=band_c, stride_axis=0)
            tiles.append(tile)
        whole = jnp.concatenate(tiles, axis=0)
        prod = [
            lax.dot_general(
                whole,
                axmat[h],
                (((1,), (1,)), ((), ())),
                precision=HIGHEST,
                preferred_element_type=jnp.float32,
            )
            for h in range(2)
        ]
        prod = jnp.where(odd_harm, prod[1], prod[0])
        a = prod[:, 0:lanes]
        b = prod[:, lanes : 2 * lanes]
        e = prod[:, 2 * lanes : 3 * lanes]
        f = pltpu.roll(e, half, 1)
        mixed = jnp.concatenate(
            [jnp.concatenate([a, e], axis=1), jnp.concatenate([b, f], axis=1)], axis=0
        )
        return dot(radmat[...], mixed)

    on_faces(lambda d: stiff_copy(d ^ 1).wait_recv())

    mass = [mass_ref[0], mass_ref[1]]

    def smooth(t, rr, ri, h):
        d_re, d_im, scale = dr[h, t], di[t], sc[h, t]
        return (d_re * rr + d_im * ri) * scale, (d_re * ri - d_im * rr) * scale

    per_group = GROUP // CHUNK
    for n in range(ct // GROUP):
        merged = jnp.where(odd_lane, scol_r[1, n], scol_r[0, n])
        for m in range(per_group):
            scol_m[n * per_group + m] = (
                merged if m == 0 else pltpu.roll(merged, lanes - 2 * CHUNK * m, 1)
            )

    def setup_step(t, u, packed, beside, moved):
        value = stiff[t + 1]
        up, dn, lo, hi = around(
            value,
            srow_r[0, pl.ds(t, 1), :],
            srow_r[1, pl.ds(t, 1), :],
            pltpu.roll(beside, lanes - 1 - 2 * u, 1),
        )
        c_up, c_dn = 0.5 * (value + up), 0.5 * (value + dn)
        c_lo, c_hi = 0.5 * (value + lo), 0.5 * (value + hi)
        c_be, c_ah = 0.5 * (value + stiff[t]), 0.5 * (value + stiff[t + 2])
        wr_up[t] = c_up
        wr_dn[t] = c_dn
        wa_lo[t] = c_lo
        wa_hi[t] = c_hi
        wt[t] = c_be
        wt[t + 1] = c_ah
        total = c_dn + c_up + c_hi + c_lo + c_ah + c_be
        density = lookup(ids_ref[t], dens_ref)
        dens[t] = density
        moved = [m + w for m, w in zip(moved, (c_up, c_dn, c_lo, c_hi, density))]
        d_im = LOSS_FACTOR * total
        di[t] = d_im
        y = [None] * 4
        for h in range(2):
            d_re = total - mass[h] * density
            scale = RELAXATION / (d_re * d_re + d_im * d_im)
            dr[h, t] = d_re
            sc[h, t] = scale
            rr, ri = rhs_ref[0, h, t], rhs_ref[1, h, t]
            y[h] = (d_re * rr + d_im * ri) * scale
            y[2 + h] = (d_re * ri - d_im * rr) * scale
            sol_ref[0, h, t] = y[h]
            sol_ref[1, h, t] = y[2 + h]
        for c in range(4):
            packed = pack(y[c], c * CHUNK + u, packed)
        return packed, moved

    def in_parts(k, step, carry):
        def one_part(part, carry):
            carry = lax.fori_loop(
                0, part_chunks, lambda n, carry: step(part * part_chunks + n, carry), carry
            )
            on_faces(lambda d: halo_copy(k, part, d).start())
            return carry

        return lax.fori_loop(0, PARTS, one_part, carry)

    def setup_chunk(chunk, moved):
        packed = zero
        beside = scol_m[chunk]
        for u in range(CHUNK):
            packed, moved = setup_step(chunk * CHUNK + u, u, packed, beside, moved)
        col_s[0, chunk] = packed
        return tuple(moved)

    moved = in_parts(0, setup_chunk, (zero,) * 5)

    trig = [[], []]
    for h in range(2):
        angle = jnp.full((rows, lanes), harm_ref[h], jnp.int32).astype(jnp.float32) * (
            2.0 * jnp.pi / NSECT
        )
        trig[0].append(jnp.cos(angle))
        trig[1].append(jnp.sin(angle))
    trig = trig[0] + trig[1]

    def load(t):
        return [sol_ref[c // 2, c % 2, t] for c in range(4)]

    def apply_operator(k):
        start = load(0)
        beyond = turn(trig, start, 1.0)
        before = turn(trig, load(ct - 1), -1.0)

        def chunk_pass(chunk, carry):
            xm, x, sums = list(carry[0:4]), list(carry[4:8]), list(carry[8:])
            beside = jnp.where(odd_lane, col_r[k, 1, chunk], col_r[k, 0, chunk])
            for c in range(4):
                for u in range(CHUNK):
                    at = c * CHUNK + u
                    edge_ref[c, u] = pltpu.roll(beside, lanes - 1 - 2 * at, 1)
            for u in range(CHUNK):
                t = chunk * CHUNK + u
                if u < CHUNK - 1:
                    xp = load(t + 1)
                else:
                    ended = t == ct - 1
                    xp = load(jnp.minimum(t + 1, ct - 1))
                    xp = [jnp.where(ended, beyond[c], xp[c]) for c in range(4)]
                c_up, c_dn, c_lo, c_hi = wr_up[t], wr_dn[t], wa_lo[t], wa_hi[t]
                c_be, c_ah = wt[t], wt[t + 1]
                nb = []
                for c in range(4):
                    up, dn, lo, hi = around(
                        x[c], row_r[k, 0, c // 2, c % 2, t], row_r[k, 1, c // 2, c % 2, t], edge_ref[c, u]
                    )
                    nb.append(
                        (c_dn * dn + c_up * up)
                        + (c_hi * hi + c_lo * lo)
                        + (c_ah * xp[c] + c_be * xm[c])
                    )
                nb = lossy(nb)
                d_im = di[t]
                for h in range(2):
                    d_re = dr[h, t]
                    re, im = h, 2 + h
                    val_re = rhs_ref[0, h, t] - (d_re * x[re] - d_im * x[im] - nb[re])
                    val_im = rhs_ref[1, h, t] - (d_re * x[im] + d_im * x[re] - nb[im])
                    val_ref[0, h, t] = val_re
                    val_ref[1, h, t] = val_im
                    sums[re] = sums[re] + val_re
                    sums[im] = sums[im] + val_im
                xm, x = x, xp
            return tuple(xm) + tuple(x) + tuple(sums)

        def one_part(part, carry):
            on_faces(lambda d: halo_copy(k, part, d ^ 1).wait_recv())
            return lax.fori_loop(
                0, part_chunks, lambda n, carry: chunk_pass(part * part_chunks + n, carry), carry
            )

        return lax.fori_loop(0, PARTS, one_part, tuple(before) + tuple(start) + (zero,) * 4)[8:]

    for k in range(ITERS):
        final = k == ITERS - 1
        sums = apply_operator(k)
        coarse = finish_coarse(k)
        corr = [coarse[c * per : c * per + rows, 0:lanes] for c in range(4)]
        apart = [[], [], [], []]
        for c in range(4):
            line = c * per + rows
            beside = coarse[c * per : c * per + rows, lanes : 2 * lanes]
            shifted = (
                jnp.where(row == 0, coarse[line : line + 1, 0:lanes], pltpu.roll(corr[c], 1, 0)),
                jnp.where(
                    row == rows - 1,
                    coarse[line + 1 : line + 2, 0:lanes],
                    pltpu.roll(corr[c], rows - 1, 0),
                ),
                jnp.where(lane == 0, beside, pltpu.roll(corr[c], 1, 1)),
                jnp.where(
                    lane == lanes - 1,
                    pltpu.roll(beside, lanes - 2, 1),
                    pltpu.roll(corr[c], lanes - 1, 1),
                ),
            )
            for n in range(4):
                apart[n].append(corr[c] - shifted[n])
        push = [lossy(apart[n]) for n in range(4)]
        push.append([mass[c % 2] * corr[c] for c in range(4)])
        ends = []
        for sign, weight in ((-1.0, wt[0]), (1.0, wt[ct])):
            over = turn(trig, corr, sign)
            ends.append([weight * x for x in lossy([corr[c] - over[c] for c in range(4)])])
        if not final:
            restrict_and_send(
                k + 1,
                [
                    sums[c] - coarse_change(moved, push, c) - ends[0][c] - ends[1][c]
                    for c in range(4)
                ],
            )
        for c in range(4):
            val_ref[c // 2, c % 2, 0] = val_ref[c // 2, c % 2, 0] - ends[0][c]
            val_ref[c // 2, c % 2, ct - 1] = val_ref[c // 2, c % 2, ct - 1] - ends[1][c]
        if final:
            for c in range(4):
                corr_ref[c] = corr[c]
                for n in range(5):
                    push_ref[n, c] = push[n][c]
            break

        @pl.loop(0, PARTS)
        def _(part):
            on_faces(lambda d: halo_copy(k, part, d).wait_send())

        def update_chunk(chunk, nothing):
            packed = zero
            for u in range(CHUNK):
                t = chunk * CHUNK + u
                weights = (wr_up[t], wr_dn[t], wa_lo[t], wa_hi[t], dens[t])
                res = [
                    val_ref[c // 2, c % 2, t] - coarse_change(weights, push, c) for c in range(4)
                ]
                x = load(t)
                y = [None] * 4
                for h in range(2):
                    a, b = smooth(t, res[h], res[2 + h], h)
                    y[h], y[2 + h] = (x[h] + corr[h]) + a, (x[2 + h] + corr[2 + h]) + b
                for c in range(4):
                    sol_ref[c // 2, c % 2, t] = y[c]
                    packed = pack(y[c], c * CHUNK + u, packed)
            col_s[k + 1, chunk] = packed
            return nothing

        in_parts(k + 1, update_chunk, 0)

    on_faces(lambda d: stiff_copy(d).wait_send())

    @pl.loop(0, PARTS)
    def _(part):
        on_faces(lambda d: halo_copy(ITERS - 1, part, d).wait_send())

    for k in range(ITERS):

        @pl.loop(1, ndev)
        def _(d):
            gather(k, d).wait_send()


def last_pass(
    sol_ref,
    val_ref,
    wr_up,
    wr_dn,
    wa_lo,
    wa_hi,
    dens,
    corr_ref,
    push_ref,
    sol_hbm,
    res_hbm,
    sol_out,
    res_out,
    sem,
):
    ct = sol_ref.shape[2]
    chunks = ct // CHUNK
    corr = [corr_ref[c] for c in range(4)]
    push = [[push_ref[n, c] for c in range(4)] for n in range(5)]

    def put(n, chunk):
        src, dst = ((sol_out, sol_hbm), (res_out, res_hbm))[n]
        at = pl.ds(chunk * CHUNK, CHUNK)
        return pltpu.make_async_copy(src.at[:, :, at], dst.at[:, :, at], sem.at[n, chunk])

    @pl.loop(0, chunks)
    def _(chunk):
        for u in range(CHUNK):
            t = chunk * CHUNK + u
            weights = (wr_up[t], wr_dn[t], wa_lo[t], wa_hi[t], dens[t])
            for c in range(4):
                sol_out[c // 2, c % 2, t] = sol_ref[c // 2, c % 2, t] + corr[c]
                res_out[c // 2, c % 2, t] = val_ref[c // 2, c % 2, t] - coarse_change(
                    weights, push, c
                )
        for n in range(2):
            put(n, chunk).start()

    @pl.loop(0, chunks)
    def _(chunk):
        for n in range(2):
            put(n, chunk).wait()


def local(rhs, mat_ids, stiff_table, dens_table, mass_shift, harmonic, radial_factor, axial_factor):
    nrad = lax.axis_size("radial")
    nax = lax.axis_size("axial")
    ct, rows, lanes = mat_ids.shape
    vmem = pl.BlockSpec(memory_space=pltpu.VMEM)
    hbm = pl.BlockSpec(memory_space=pltpu.HBM)
    f32 = jnp.float32
    field = (ct, rows, lanes)
    chunks = ct // CHUNK
    groups = ct // GROUP
    cdev = 4 * (rows // AR)
    ndev = nrad * nax
    dma = pltpu.SemaphoreType.DMA
    inputs = (
        rhs,
        mat_ids,
        stiff_table,
        dens_table,
        mass_shift,
        harmonic,
        radial_factor,
        axial_factor,
    )
    held = (
        rhs.shape,
        rhs.shape,
        field,
        field,
        field,
        field,
        field,
        (4, rows, lanes),
        (5, 4, rows, lanes),
    )
    state = pl.pallas_call(
        functools.partial(kernel, nrad, nax),
        out_shape=tuple(pltpu.VMEM(shape, f32) for shape in held),
        in_specs=[hbm] * 8,
        out_specs=(vmem,) * len(held),
        scratch_shapes=[
            pltpu.VMEM(rhs.shape, f32),
            pltpu.VMEM(field, jnp.int32),
            pltpu.SMEM(stiff_table.shape, f32),
            pltpu.SMEM(dens_table.shape, f32),
            pltpu.SMEM(mass_shift.shape, f32),
            pltpu.SMEM(harmonic.shape, jnp.int32),
            pltpu.VMEM(radial_factor.shape, f32),
            pltpu.VMEM(axial_factor.shape, f32),
            dma((8,)),
            pltpu.VMEM((ct + 2, rows, lanes), f32),
            pltpu.VMEM((ct + 1, rows, lanes), f32),
            pltpu.VMEM((2,) + field, f32),
            pltpu.VMEM(field, f32),
            pltpu.VMEM((2,) + field, f32),
            pltpu.VMEM((4, CHUNK, rows, lanes), f32),
            pltpu.VMEM((2, ct, lanes), f32),
            pltpu.VMEM((2, ct, lanes), f32),
            pltpu.VMEM((groups, rows, lanes), f32),
            pltpu.VMEM((2, groups, rows, lanes), f32),
            pltpu.VMEM((chunks, rows, lanes), f32),
            pltpu.VMEM((ITERS, 2, 2, 2, ct, 1, lanes), f32),
            pltpu.VMEM((ITERS, chunks, rows, lanes), f32),
            pltpu.VMEM((ITERS, 2, chunks, rows, lanes), f32),
            pltpu.VMEM((ITERS, ndev, 1, lanes), f32),
            pltpu.VMEM((2, 3 * lanes, lanes), f32),
            pltpu.VMEM((8 * rows, 2 * nrad * cdev), f32),
            dma((4,)),
            dma((4,)),
            dma((ITERS, PARTS, 4)),
            dma((ITERS, PARTS, 4)),
            dma((ITERS, ndev)),
            dma((ITERS, ndev)),
        ],
        compiler_params=pltpu.CompilerParams(
            collective_id=0, has_side_effects=True, vmem_limit_bytes=48 * 1024 * 1024
        ),
    )(*[pltpu.with_memory_space_constraint(x, pltpu.HBM) for x in inputs])
    return pl.pallas_call(
        last_pass,
        out_shape=(jax.ShapeDtypeStruct(rhs.shape, f32), jax.ShapeDtypeStruct(rhs.shape, f32)),
        in_specs=[vmem] * len(held),
        out_specs=(hbm, hbm),
        scratch_shapes=[
            pltpu.VMEM(rhs.shape, f32),
            pltpu.VMEM(rhs.shape, f32),
            dma((2, chunks)),
        ],
        compiler_params=pltpu.CompilerParams(vmem_limit_bytes=32 * 1024 * 1024),
    )(*[pltpu.with_memory_space_constraint(x, pltpu.VMEM) for x in state])


def solution(mesh):
    return jax.shard_map(
        local,
        mesh=mesh,
        in_specs=(
            P(None, None, None, "radial", "axial"),
            P(None, "radial", "axial"),
            P(),
            P(),
            P(),
            P(),
            P(),
            P(),
        ),
        out_specs=(P(None, None, None, "radial", "axial"), P(None, None, None, "radial", "axial")),
        check_vma=False,
    )
```

time: 50.1 us -> 42 us (0.84)
  the two profiles are of different devices: /device:TPU:1 before, /device:TPU:3 now
where the time goes in v2:
time: 42 us; the launch traced here: 41.8 us
  Pallas kernels  41.2 us (98%)
  between operations  0.64 us (2%)
    pallas_call x1, Pallas kernels, local(): pl.pallas_call(functools.partial(kernel, nrad, nax), out_shape=tuple((plt...  39.3 us
    pallas_call x1, Pallas kernels, local(): pl.pallas_call(last_pass, out_shape=(jax.ShapeDtypeStruct(rhs.shape, f32)...  1.87 us

profile of v2, /device:TPU:3, one launch (start us, length us, event | category | flops | bytes accessed | tf_op | source)
XLA Modules:
  0.0 41.8 jit_solution(5768690711631179068)
XLA Ops:
  0.6 39.3 %shard_map.95 = (f32[2,2,96,8,128]{4,3,2,1,0:T(8,128)S(1)}, f32[2,2,96,8,128]{4,3,2,1,0:T(8,128)S(1)}, f32[96,8,128]{2,1,0:T(8,128)S(1)}, f32[96,8,128]{2,1,0:T(...) custom-call(f32[2,2,96,8,128]{4,3,2,1,0:T(8,128)} %rhs_hbm.1, ...), custom_call_target="tpu_custom_call" | custom-call | tf_op jit(solution)/shard_map/pallas_call | solution.py:676
  40.0 1.9 %shard_map.96 = (f32[2,2,96,8,128]{4,3,2,1,0:T(8,128)}, f32[2,2,96,8,128]{4,3,2,1,0:T(8,128)}) custom-call(f32[2,2,96,8,128]{4,3,2,1,0:T(8,128)S(1)} %get-tuple-element.11.sol_ref, f32[2,2,96,8,128]{4,3,2,1,0:T(8,128)S(1)} %get-tuple-element.12.val_ref, f32[96,8,128]{2,1,0:T(8,128)S(1)} %get-tuple-element.13.wr_up, ...), custom_call_target="tpu_custom_call" | custom-call | tf_op jit(solution)/shard_map/pallas_call | solution.py:719

commit v3 on v2

--- a/solution.py
+++ b/solution.py
@@ -40,6 +40,18 @@
         pltpu.roll(jnp.where(lane == lanes - 1, edge, value), 1, 1),
         pltpu.roll(jnp.where(lane == 0, edge, value), lanes - 1, 1),
     )
+
+
+def face_terms(fix_rows, fix_cols, t, chunk, c, u):
+    rows, lanes = fix_cols.shape[1:]
+    row, lane = grid_of(rows, lanes)
+    edge = pltpu.roll(fix_cols[chunk], lanes - 1 - 2 * (c * CHUNK + u), 1)
+    along = jnp.where(
+        row == 0,
+        fix_rows[0, c, pl.ds(t, 1), :],
+        jnp.where(row == rows - 1, fix_rows[1, c, pl.ds(t, 1), :], 0.0),
+    )
+    return along + jnp.where((lane == 0) | (lane == lanes - 1), edge, 0.0)
 
 
 def lossy(x):
@@ -82,6 +94,8 @@
     dens,
     corr_ref,
     push_ref,
+    fix_rows,
+    fix_cols,
     rhs_ref,
     ids_ref,
     stiff_ref,
@@ -96,7 +110,8 @@
     dr,
     di,
     sc,
-    edge_ref,
+    w_rows,
+    w_cols,
     srow_s,
     srow_r,
     scol_s,
@@ -205,7 +220,7 @@
     def halo_copy(k, part, d):
         if d < 2:
             at = pl.ds(part * part_ct, part_ct)
-            line = pl.ds(0 if d == 0 else rows - 1, 1)
+            line = 0 if d == 0 else rows - 1
             src, dst = sol_ref.at[:, :, at, line], row_r.at[k, 1 - d, :, :, at]
         else:
             at = pl.ds(part * part_chunks, part_chunks)
@@ -383,7 +398,7 @@
                 merged if m == 0 else pltpu.roll(merged, lanes - 2 * CHUNK * m, 1)
             )
 
-    def setup_step(t, u, packed, beside, moved):
+    def setup_step(t, u, packed, faces, beside, moved):
         value = stiff[t + 1]
         up, dn, lo, hi = around(
             value,
@@ -398,6 +413,8 @@
         wr_dn[t] = c_dn
         wa_lo[t] = c_lo
         wa_hi[t] = c_hi
+        w_rows[0, pl.ds(t, 1), :] = c_up[0:1]
+        w_rows[1, pl.ds(t, 1), :] = c_dn[rows - 1 : rows]
         wt[t] = c_be
         wt[t + 1] = c_ah
         total = c_dn + c_up + c_hi + c_lo + c_ah + c_be
@@ -419,12 +436,17 @@
             sol_ref[1, h, t] = y[2 + h]
         for c in range(4):
             packed = pack(y[c], c * CHUNK + u, packed)
-        return packed, moved
+        faces = pack(jnp.where(lane == 0, c_lo, c_hi), u, faces)
+        return packed, faces, moved
 
     def in_parts(k, step, carry):
         def one_part(part, carry):
             carry = lax.fori_loop(
-                0, part_chunks, lambda n, carry: step(part * part_chunks + n, carry), carry
+                0,
+                part_chunks,
+                lambda n, carry: step(part * part_chunks + n, carry),
+                carry,
+                unroll=True,
             )
             on_faces(lambda d: halo_copy(k, part, d).start())
             return carry
@@ -433,10 +455,13 @@
 
     def setup_chunk(chunk, moved):
         packed = zero
+        faces = zero
         beside = scol_m[chunk]
         for u in range(CHUNK):
-            packed, moved = setup_step(chunk * CHUNK + u, u, packed, beside, moved)
+            packed, faces, moved = setup_step(chunk * CHUNK + u, u, packed, faces, beside, moved)
         col_s[0, chunk] = packed
+        faces = faces + pltpu.roll(faces, 2 * CHUNK, 1)
+        w_cols[chunk] = faces + pltpu.roll(faces, 4 * CHUNK, 1)
         return tuple(moved)
 
     moved = in_parts(0, setup_chunk, (zero,) * 5)
@@ -460,11 +485,6 @@
 
         def chunk_pass(chunk, carry):
             xm, x, sums = list(carry[0:4]), list(carry[4:8]), list(carry[8:])
-            beside = jnp.where(odd_lane, col_r[k, 1, chunk], col_r[k, 0, chunk])
-            for c in range(4):
-                for u in range(CHUNK):
-                    at = c * CHUNK + u
-                    edge_ref[c, u] = pltpu.roll(beside, lanes - 1 - 2 * at, 1)
             for u in range(CHUNK):
                 t = chunk * CHUNK + u
                 if u < CHUNK - 1:
@@ -477,9 +497,10 @@
                 c_be, c_ah = wt[t], wt[t + 1]
                 nb = []
                 for c in range(4):
-                    up, dn, lo, hi = around(
-                        x[c], row_r[k, 0, c // 2, c % 2, t], row_r[k, 1, c // 2, c % 2, t], edge_ref[c, u]
-                    )
+                    up = jnp.where(row == 0, 0.0, pltpu.roll(x[c], 1, 0))
+                    dn = jnp.where(row == rows - 1, 0.0, pltpu.roll(x[c], rows - 1, 0))
+                    lo = jnp.where(lane == 0, 0.0, pltpu.roll(x[c], 1, 1))
+                    hi = jnp.where(lane == lanes - 1, 0.0, pltpu.roll(x[c], lanes - 1, 1))
                     nb.append(
                         (c_dn * dn + c_up * up)
                         + (c_hi * hi + c_lo * lo)
@@ -499,13 +520,53 @@
                 xm, x = x, xp
             return tuple(xm) + tuple(x) + tuple(sums)
 
-        def one_part(part, carry):
+        carry = tuple(before) + tuple(start) + (zero,) * 4
+        return lax.fori_loop(0, chunks, chunk_pass, carry, unroll=4)[8:]
+
+    def fix_faces(k, sums):
+        @pl.loop(0, PARTS)
+        def _(part):
             on_faces(lambda d: halo_copy(k, part, d ^ 1).wait_recv())
-            return lax.fori_loop(
-                0, part_chunks, lambda n, carry: chunk_pass(part * part_chunks + n, carry), carry
+
+        def chunk_fix(chunk, carry):
+            out = []
+            at = pl.ds(pl.multiple_of(chunk * CHUNK, CHUNK), CHUNK)
+            for side in range(2):
+                weight = w_rows[side, at]
+                term = lossy([weight * row_r[k, side, c // 2, c % 2, at] for c in range(4)])
+                for c in range(4):
+                    fix_rows[side, c, at] = term[c]
+                    out.append(carry[4 * side + c] + term[c])
+            term = w_cols[chunk] * jnp.where(
+                odd_lane,
+                pltpu.roll(col_r[k, 0, chunk], 1, 1),
+                pltpu.roll(col_r[k, 1, chunk], lanes - 1, 1),
             )
-
-        return lax.fori_loop(0, PARTS, one_part, tuple(before) + tuple(start) + (zero,) * 4)[8:]
+            turned = jnp.where(
+                pair < 2 * CHUNK,
+                -pltpu.roll(term, lanes - 4 * CHUNK, 1),
+                pltpu.roll(term, 4 * CHUNK, 1),
+            )
+            term = term + LOSS_FACTOR * turned
+            fix_cols[chunk] = term
+            return tuple(out) + (carry[8] + term,)
+
+        carry = lax.fori_loop(0, chunks, chunk_fix, (zero,) * 9, unroll=4)
+        beside = carry[8]
+        step = 1
+        while step < CHUNK:
+            beside = beside + pltpu.roll(beside, lanes - 2 * step, 1)
+            step *= 2
+        outs = []
+        for c in range(4):
+            edge = pltpu.roll(beside, lanes - 1 - 2 * c * CHUNK, 1)
+            outs.append(
+                sums[c]
+                + jnp.where(row == 0, jnp.sum(carry[c], axis=0, keepdims=True), 0.0)
+                + jnp.where(row == rows - 1, jnp.sum(carry[4 + c], axis=0, keepdims=True), 0.0)
+                + jnp.where((lane == 0) | (lane == lanes - 1), edge, 0.0)
+            )
+        return outs
 
     for k in range(ITERS):
         final = k == ITERS - 1
@@ -538,6 +599,7 @@
         for sign, weight in ((-1.0, wt[0]), (1.0, wt[ct])):
             over = turn(trig, corr, sign)
             ends.append([weight * x for x in lossy([corr[c] - over[c] for c in range(4)])])
+        sums = fix_faces(k, sums)
         if not final:
             restrict_and_send(
                 k + 1,
@@ -566,7 +628,9 @@
                 t = chunk * CHUNK + u
                 weights = (wr_up[t], wr_dn[t], wa_lo[t], wa_hi[t], dens[t])
                 res = [
-                    val_ref[c // 2, c % 2, t] - coarse_change(weights, push, c) for c in range(4)
+                    (val_ref[c // 2, c % 2, t] - coarse_change(weights, push, c))
+                    + face_terms(fix_rows, fix_cols, t, chunk, c, u)
+                    for c in range(4)
                 ]
                 x = load(t)
                 y = [None] * 4
@@ -604,6 +668,8 @@
     dens,
     corr_ref,
     push_ref,
+    fix_rows,
+    fix_cols,
     sol_hbm,
     res_hbm,
     sol_out,
@@ -627,9 +693,9 @@
             weights = (wr_up[t], wr_dn[t], wa_lo[t], wa_hi[t], dens[t])
             for c in range(4):
                 sol_out[c // 2, c % 2, t] = sol_ref[c // 2, c % 2, t] + corr[c]
-                res_out[c // 2, c % 2, t] = val_ref[c // 2, c % 2, t] - coarse_change(
-                    weights, push, c
-                )
+                res_out[c // 2, c % 2, t] = (
+                    val_ref[c // 2, c % 2, t] - coarse_change(weights, push, c)
+                ) + face_terms(fix_rows, fix_cols, t, chunk, c, u)
         for n in range(2):
             put(n, chunk).start()
 
@@ -672,6 +738,8 @@
         field,
         (4, rows, lanes),
         (5, 4, rows, lanes),
+        (2, 4, ct, lanes),
+        (chunks, rows, lanes),
     )
     state = pl.pallas_call(
         functools.partial(kernel, nrad, nax),
@@ -693,13 +761,14 @@
             pltpu.VMEM((2,) + field, f32),
             pltpu.VMEM(field, f32),
             pltpu.VMEM((2,) + field, f32),
-            pltpu.VMEM((4, CHUNK, rows, lanes), f32),
+            pltpu.VMEM((2, ct, lanes), f32),
+            pltpu.VMEM((chunks, rows, lanes), f32),
             pltpu.VMEM((2, ct, lanes), f32),
             pltpu.VMEM((2, ct, lanes), f32),
             pltpu.VMEM((groups, rows, lanes), f32),
             pltpu.VMEM((2, groups, rows, lanes), f32),
             pltpu.VMEM((chunks, rows, lanes), f32),
-            pltpu.VMEM((ITERS, 2, 2, 2, ct, 1, lanes), f32),
+            pltpu.VMEM((ITERS, 2, 2, 2, ct, lanes), f32),
             pltpu.VMEM((ITERS, chunks, rows, lanes), f32),
             pltpu.VMEM((ITERS, 2, chunks, rows, lanes), f32),
             pltpu.VMEM((ITERS, ndev, 1, lanes), f32),

time: 42 us -> 38.3 us (0.912)
  the two profiles are of different devices: /device:TPU:3 before, /device:TPU:1 now
where the time goes in v3:
time: 38.3 us; the launch traced here: 38.2 us
  Pallas kernels  37.5 us (98%)
  between operations  0.64 us (2%)
    pallas_call x1, Pallas kernels, local(): pl.pallas_call(functools.partial(kernel, nrad, nax), out_shape=tuple((plt...  35.3 us
    pallas_call x1, Pallas kernels, local(): pl.pallas_call(last_pass, out_shape=(jax.ShapeDtypeStruct(rhs.shape, f32)...  2.2 us

profile of v3, /device:TPU:1, one launch (start us, length us, event | category | flops | bytes accessed | tf_op | source)
XLA Modules:
  0.0 38.2 jit_solution(13717958316675687442)
XLA Ops:
  0.6 35.3 %shard_map.95 = (f32[2,2,96,8,128]{4,3,2,1,0:T(8,128)S(1)}, f32[2,2,96,8,128]{4,3,2,1,0:T(8,128)S(1)}, f32[96,8,128]{2,1,0:T(8,128)S(1)}, f32[96,8,128]{2,1,0:T(...) custom-call(f32[2,2,96,8,128]{4,3,2,1,0:T(8,128)} %rhs_hbm.1, ...), custom_call_target="tpu_custom_call" | custom-call | tf_op jit(solution)/shard_map/pallas_call | solution.py:744
  36.0 2.2 %shard_map.96 = (f32[2,2,96,8,128]{4,3,2,1,0:T(8,128)}, f32[2,2,96,8,128]{4,3,2,1,0:T(8,128)}) custom-call(f32[2,2,96,8,128]{4,3,2,1,0:T(8,128)S(1)} %get-tuple-element.13.sol_ref, f32[2,2,96,8,128]{4,3,2,1,0:T(8,128)S(1)} %get-tuple-element.14.val_ref, f32[96,8,128]{2,1,0:T(8,128)S(1)} %get-tuple-element.15.wr_up, ...), custom_call_target="tpu_custom_call" | custom-call | tf_op jit(solution)/shard_map/pallas_call | solution.py:788

commit v4 on v3

--- a/solution.py
+++ b/solution.py
@@ -163,15 +163,27 @@
     conds = (has_up, has_dn, has_lo, has_hi)
     targets = ({"radial": i - 1}, {"radial": i + 1}, {"axial": j - 1}, {"axial": j + 1})
 
-    def peer(d):
-        at = lax.rem(me + d, ndev)
-        return {"radial": at // nax, "axial": lax.rem(at, nax)}
+    def each_peer(act):
+        def along(a):
+            to = i + a
+            to = jnp.where(to >= nrad, to - nrad, to)
+            for b in range(nax):
+                at = j + b
+                act({"radial": to, "axial": jnp.where(at >= nax, at - nax, at)})
+
+        for b in range(1, nax):
+            at = j + b
+            act({"radial": i, "axial": jnp.where(at >= nax, at - nax, at)})
+        if nrad <= 8:
+            for a in range(1, nrad):
+                along(a)
+        else:
+            pl.loop(1, nrad)(along)
 
     barrier = pltpu.get_barrier_semaphore()
-
-    @pl.loop(1, ndev)
-    def _(d):
-        pl.semaphore_signal(barrier, inc=1, device_id=peer(d), device_id_type=MESH)
+    each_peer(
+        lambda peer: pl.semaphore_signal(barrier, inc=1, device_id=peer, device_id_type=MESH)
+    )
 
     for d in range(4):
 
@@ -234,15 +246,19 @@
             device_id_type=MESH,
         )
 
-    def gather(k, d):
+    def gather(k, peer):
         return pltpu.make_async_remote_copy(
             src_ref=all_r.at[k, me],
             dst_ref=all_r.at[k, me],
-            send_sem=ga_send.at[k, d],
-            recv_sem=ga_recv.at[k, d],
-            device_id=peer(d),
+            send_sem=ga_send.at[k],
+            recv_sem=ga_recv.at[k],
+            device_id=peer,
             device_id_type=MESH,
         )
+
+    def gathered(k, sem):
+        others = all_r.at[k, pl.ds(1, ndev - 1)]
+        pltpu.make_async_copy(others, others, sem.at[k]).wait()
 
     def on_faces(act):
         for d in range(4):
@@ -280,10 +296,7 @@
     def restrict_and_send(k, sums):
         folded = dot(jnp.concatenate(sums, axis=0), fold)
         all_r[k, me] = jnp.sum(jnp.where(keep, folded, 0.0), axis=0, keepdims=True)
-
-        @pl.loop(1, ndev)
-        def _(d):
-            gather(k, d).start()
+        each_peer(lambda peer: gather(k, peer).start())
 
     loads[2].wait()
 
@@ -350,9 +363,7 @@
     odd_harm = (p_row // band_r) % 2 == 1
 
     def finish_coarse(k):
-        @pl.loop(1, ndev)
-        def _(d):
-            gather(k, d).wait_recv()
+        gathered(k, ga_recv)
 
         tiles = []
         for a in range(nrad):
@@ -652,10 +663,7 @@
         on_faces(lambda d: halo_copy(ITERS - 1, part, d).wait_send())
 
     for k in range(ITERS):
-
-        @pl.loop(1, ndev)
-        def _(d):
-            gather(k, d).wait_send()
+        gathered(k, ga_send)
 
 
 def last_pass(
@@ -778,8 +786,8 @@
             dma((4,)),
             dma((ITERS, PARTS, 4)),
             dma((ITERS, PARTS, 4)),
-            dma((ITERS, ndev)),
-            dma((ITERS, ndev)),
+            dma((ITERS,)),
+            dma((ITERS,)),
         ],
         compiler_params=pltpu.CompilerParams(
             collective_id=0, has_side_effects=True, vmem_limit_bytes=48 * 1024 * 1024

time: 38.3 us -> 35.7 us (0.932)
  Pallas kernels: 37.5 us -> 34.9 us
    pallas_call x1, Pallas kernels: 35.3 us -> 32.7 us  [local(): pl.pallas_call(functools.partial(kernel, nrad, nax), out_shape=tuple((plt...]
where the time goes in v4:
time: 35.7 us; the launch traced here: 35.5 us
  Pallas kernels  34.9 us (98%)
  between operations  0.64 us (2%)
    pallas_call x1, Pallas kernels, local(): pl.pallas_call(functools.partial(kernel, nrad, nax), out_shape=tuple((plt...  32.7 us
    pallas_call x1, Pallas kernels, local(): pl.pallas_call(last_pass, out_shape=(jax.ShapeDtypeStruct(rhs.shape, f32)...  2.2 us

profile of v4, /device:TPU:1, one launch (start us, length us, event | category | flops | bytes accessed | tf_op | source)
XLA Modules:
  0.0 35.5 jit_solution(10995035284185087802)
XLA Ops:
  0.6 32.7 %shard_map.95 = (f32[2,2,96,8,128]{4,3,2,1,0:T(8,128)S(1)}, f32[2,2,96,8,128]{4,3,2,1,0:T(8,128)S(1)}, f32[96,8,128]{2,1,0:T(8,128)S(1)}, f32[96,8,128]{2,1,0:T(...) custom-call(f32[2,2,96,8,128]{4,3,2,1,0:T(8,128)} %rhs_hbm.1, ...), custom_call_target="tpu_custom_call" | custom-call | tf_op jit(solution)/shard_map/pallas_call | solution.py:752
  33.3 2.2 %shard_map.96 = (f32[2,2,96,8,128]{4,3,2,1,0:T(8,128)}, f32[2,2,96,8,128]{4,3,2,1,0:T(8,128)}) custom-call(f32[2,2,96,8,128]{4,3,2,1,0:T(8,128)S(1)} %get-tuple-element.13.sol_ref, f32[2,2,96,8,128]{4,3,2,1,0:T(8,128)S(1)} %get-tuple-element.14.val_ref, f32[96,8,128]{2,1,0:T(8,128)S(1)} %get-tuple-element.15.wr_up, ...), custom_call_target="tpu_custom_call" | custom-call | tf_op jit(solution)/shard_map/pallas_call | solution.py:796

commit v5 on v4

--- a/solution.py
+++ b/solution.py
@@ -16,12 +16,31 @@
 MESH = pl.DeviceIdType.MESH
 HIGHEST = lax.Precision.HIGHEST
 CHUNK = 8
-PARTS = 4
+PARTS = 6
 GROUP = 32
 
 
 def dot(a, b):
     return jnp.dot(a, b, precision=HIGHEST, preferred_element_type=jnp.float32)
+
+
+def dot16(a, b):
+    return jnp.dot(a, b, preferred_element_type=jnp.float32)
+
+
+def split(x):
+    high = x.astype(jnp.bfloat16)
+    return high, (x - high.astype(jnp.float32)).astype(jnp.bfloat16)
+
+
+def left_parts(x):
+    high, low = split(x)
+    return jnp.concatenate([high, low, high], axis=1)
+
+
+def right_parts(x, axis):
+    high, low = split(x)
+    return jnp.concatenate([high, high, low], axis=axis)
 
 
 def grid_of(rows, lanes):
@@ -240,11 +259,15 @@
         return pltpu.make_async_remote_copy(
             src_ref=src,
             dst_ref=dst,
-            send_sem=ha_send.at[k, part, d],
-            recv_sem=ha_recv.at[k, part, d ^ 1],
+            send_sem=ha_send.at[k, d],
+            recv_sem=ha_recv.at[k, d ^ 1],
             device_id=targets[d],
             device_id_type=MESH,
         )
+
+    def halo_done(k, d, sem):
+        got = row_r.at[k, d] if d < 2 else col_r.at[k, d - 2]
+        pltpu.make_async_copy(got, got, sem.at[k, d]).wait()
 
     def gather(k, peer):
         return pltpu.make_async_remote_copy(
@@ -289,12 +312,13 @@
     on_faces(lambda d: stiff_copy(d).start())
 
     e_row, e_col = grid_of(lanes, lanes)
-    fold = jnp.where(e_row // AA == e_col % band_c, 1.0, 0.0)
+    fold = jnp.where(e_row // AA == e_col % band_c, 1.0, 0.0).astype(jnp.bfloat16)
+    fold = jnp.concatenate([fold, fold], axis=0)
     k_row, k_col = grid_of(4 * rows, lanes)
     keep = k_row // AR == (j + rows - k_col // band_c) % rows
 
     def restrict_and_send(k, sums):
-        folded = dot(jnp.concatenate(sums, axis=0), fold)
+        folded = dot16(jnp.concatenate(split(jnp.concatenate(sums, axis=0)), axis=1), fold)
         all_r[k, me] = jnp.sum(jnp.where(keep, folded, 0.0), axis=0, keepdims=True)
         each_peer(lambda peer: gather(k, peer).start())
 
@@ -316,14 +340,17 @@
     half = lanes // 2
     side = jnp.where(ax_row % 2 == 0, j * band_c - 1, (j + 1) * band_c) == ax_col
     edges = [jnp.where(side & (ax_row // half == p), 1.0, 0.0) for p in range(2)]
+    spare = [jnp.zeros((3 * lanes, lanes - ga), jnp.float32)] if ga < lanes else []
     for h in range(2):
-        if ga < lanes:
-            axmat[h] = jnp.zeros(axmat.shape[1:], jnp.float32)
-        axmat[h, 0:lanes, 0:ga] = dot(own, axial_ref[0, h])
-        axmat[h, lanes : 2 * lanes, 0:ga] = dot(own, axial_ref[1, h])
-        axmat[h, 2 * lanes : 3 * lanes, 0:ga] = dot(edges[0], axial_ref[0, h]) + dot(
-            edges[1], axial_ref[1, h]
+        wide = jnp.concatenate(
+            [
+                dot(own, axial_ref[0, h]),
+                dot(own, axial_ref[1, h]),
+                dot(edges[0], axial_ref[0, h]) + dot(edges[1], axial_ref[1, h]),
+            ],
+            axis=0,
         )
+        axmat[h] = right_parts(jnp.concatenate([wide] + spare, axis=1), 1)
 
     per = 2 * rows
     cdev = 4 * band_r
@@ -356,8 +383,7 @@
         second = jnp.where(same, -imag, second)
         second = jnp.where(to_re, -real, second)
         second = jnp.where(to_im, real, second)
-    radmat[:, 0 : nrad * cdev] = first
-    radmat[:, nrad * cdev : 2 * nrad * cdev] = second
+    radmat[...] = left_parts(jnp.concatenate([first, second], axis=1))
 
     p_row, _ = grid_of(nrad * cdev, 3 * lanes)
     odd_harm = (p_row // band_r) % 2 == 1
@@ -372,13 +398,12 @@
                 tile = jnp.where((lane // band_c + row) % rows == b, all_r[k, a * nax + b], tile)
             tile = pltpu.roll(tile, 0, 1, stride=band_c, stride_axis=0)
             tiles.append(tile)
-        whole = jnp.concatenate(tiles, axis=0)
+        whole = left_parts(jnp.concatenate(tiles, axis=0))
         prod = [
             lax.dot_general(
                 whole,
                 axmat[h],
                 (((1,), (1,)), ((), ())),
-                precision=HIGHEST,
                 preferred_element_type=jnp.float32,
             )
             for h in range(2)
@@ -391,7 +416,7 @@
         mixed = jnp.concatenate(
             [jnp.concatenate([a, e], axis=1), jnp.concatenate([b, f], axis=1)], axis=0
         )
-        return dot(radmat[...], mixed)
+        return dot16(radmat[...], right_parts(mixed, 0))
 
     on_faces(lambda d: stiff_copy(d ^ 1).wait_recv())
 
@@ -532,12 +557,10 @@
             return tuple(xm) + tuple(x) + tuple(sums)
 
         carry = tuple(before) + tuple(start) + (zero,) * 4
-        return lax.fori_loop(0, chunks, chunk_pass, carry, unroll=4)[8:]
+        return lax.fori_loop(0, chunks, chunk_pass, carry, unroll=3)[8:]
 
     def fix_faces(k, sums):
-        @pl.loop(0, PARTS)
-        def _(part):
-            on_faces(lambda d: halo_copy(k, part, d ^ 1).wait_recv())
+        on_faces(lambda d: halo_done(k, d, ha_recv))
 
         def chunk_fix(chunk, carry):
             out = []
@@ -562,7 +585,7 @@
             fix_cols[chunk] = term
             return tuple(out) + (carry[8] + term,)
 
-        carry = lax.fori_loop(0, chunks, chunk_fix, (zero,) * 9, unroll=4)
+        carry = lax.fori_loop(0, chunks, chunk_fix, (zero,) * 9, unroll=6)
         beside = carry[8]
         step = 1
         while step < CHUNK:
@@ -629,9 +652,7 @@
                     push_ref[n, c] = push[n][c]
             break
 
-        @pl.loop(0, PARTS)
-        def _(part):
-            on_faces(lambda d: halo_copy(k, part, d).wait_send())
+        on_faces(lambda d: halo_done(k, d, ha_send))
 
         def update_chunk(chunk, nothing):
             packed = zero
@@ -658,9 +679,7 @@
 
     on_faces(lambda d: stiff_copy(d).wait_send())
 
-    @pl.loop(0, PARTS)
-    def _(part):
-        on_faces(lambda d: halo_copy(ITERS - 1, part, d).wait_send())
+    on_faces(lambda d: halo_done(ITERS - 1, d, ha_send))
 
     for k in range(ITERS):
         gathered(k, ga_send)
@@ -780,12 +799,12 @@
             pltpu.VMEM((ITERS, chunks, rows, lanes), f32),
             pltpu.VMEM((ITERS, 2, chunks, rows, lanes), f32),
             pltpu.VMEM((ITERS, ndev, 1, lanes), f32),
-            pltpu.VMEM((2, 3 * lanes, lanes), f32),
-            pltpu.VMEM((8 * rows, 2 * nrad * cdev), f32),
+            pltpu.VMEM((2, 3 * lanes, 3 * lanes), jnp.bfloat16),
+            pltpu.VMEM((8 * rows, 6 * nrad * cdev), jnp.bfloat16),
             dma((4,)),
             dma((4,)),
-            dma((ITERS, PARTS, 4)),
-            dma((ITERS, PARTS, 4)),
+            dma((ITERS, 4)),
+            dma((ITERS, 4)),
             dma((ITERS,)),
             dma((ITERS,)),
         ],

time: 35.7 us -> 33.1 us (0.927)
  Pallas kernels: 34.9 us -> 32.3 us
    pallas_call x1, Pallas kernels: 32.7 us -> 30.1 us  [local(): pl.pallas_call(functools.partial(kernel, nrad, nax), out_shape=tuple((plt...]
where the time goes in v5:
time: 33.1 us; the launch traced here: 33 us
  Pallas kernels  32.3 us (98%)
  between operations  0.64 us (2%)
    pallas_call x1, Pallas kernels, local(): pl.pallas_call(functools.partial(kernel, nrad, nax), out_shape=tuple((plt...  30.1 us
    pallas_call x1, Pallas kernels, local(): pl.pallas_call(last_pass, out_shape=(jax.ShapeDtypeStruct(rhs.shape, f32)...  2.2 us

profile of v5, /device:TPU:1, one launch (start us, length us, event | category | flops | bytes accessed | tf_op | source)
XLA Modules:
  0.0 33.0 jit_solution(10158371425385953628)
XLA Ops:
  0.6 30.1 %shard_map.95 = (f32[2,2,96,8,128]{4,3,2,1,0:T(8,128)S(1)}, f32[2,2,96,8,128]{4,3,2,1,0:T(8,128)S(1)}, f32[96,8,128]{2,1,0:T(8,128)S(1)}, f32[96,8,128]{2,1,0:T(...) custom-call(f32[2,2,96,8,128]{4,3,2,1,0:T(8,128)} %rhs_hbm.1, ...), custom_call_target="tpu_custom_call" | custom-call | tf_op jit(solution)/shard_map/pallas_call | solution.py:771
  30.8 2.2 %shard_map.96 = (f32[2,2,96,8,128]{4,3,2,1,0:T(8,128)}, f32[2,2,96,8,128]{4,3,2,1,0:T(8,128)}) custom-call(f32[2,2,96,8,128]{4,3,2,1,0:T(8,128)S(1)} %get-tuple-element.13.sol_ref, f32[2,2,96,8,128]{4,3,2,1,0:T(8,128)S(1)} %get-tuple-element.14.val_ref, f32[96,8,128]{2,1,0:T(8,128)S(1)} %get-tuple-element.15.wr_up, ...), custom_call_target="tpu_custom_call" | custom-call | tf_op jit(solution)/shard_map/pallas_call | solution.py:815

commit v6 on v5

--- a/solution.py
+++ b/solution.py
@@ -418,6 +418,15 @@
         )
         return dot16(radmat[...], right_parts(mixed, 0))
 
+    trig = [[], []]
+    for h in range(2):
+        angle = jnp.full((rows, lanes), harm_ref[h], jnp.int32).astype(jnp.float32) * (
+            2.0 * jnp.pi / NSECT
+        )
+        trig[0].append(jnp.cos(angle))
+        trig[1].append(jnp.sin(angle))
+    trig = trig[0] + trig[1]
+
     on_faces(lambda d: stiff_copy(d ^ 1).wait_recv())
 
     mass = [mass_ref[0], mass_ref[1]]
@@ -502,14 +511,6 @@
 
     moved = in_parts(0, setup_chunk, (zero,) * 5)
 
-    trig = [[], []]
-    for h in range(2):
-        angle = jnp.full((rows, lanes), harm_ref[h], jnp.int32).astype(jnp.float32) * (
-            2.0 * jnp.pi / NSECT
-        )
-        trig[0].append(jnp.cos(angle))
-        trig[1].append(jnp.sin(angle))
-    trig = trig[0] + trig[1]
 
     def load(t):
         return [sol_ref[c // 2, c % 2, t] for c in range(4)]
@@ -585,7 +586,7 @@
             fix_cols[chunk] = term
             return tuple(out) + (carry[8] + term,)
 
-        carry = lax.fori_loop(0, chunks, chunk_fix, (zero,) * 9, unroll=6)
+        carry = lax.fori_loop(0, chunks, chunk_fix, (zero,) * 9, unroll=12)
         beside = carry[8]
         step = 1
         while step < CHUNK:
@@ -713,7 +714,7 @@
         at = pl.ds(chunk * CHUNK, CHUNK)
         return pltpu.make_async_copy(src.at[:, :, at], dst.at[:, :, at], sem.at[n, chunk])
 
-    @pl.loop(0, chunks)
+    @pl.loop(0, chunks, unroll=3)
     def _(chunk):
         for u in range(CHUNK):
             t = chunk * CHUNK + u

time: 33.1 us -> 32.4 us (0.979)
  Pallas kernels: 32.3 us -> 31.6 us
    pallas_call x1, Pallas kernels: 30.1 us -> 29.6 us  [local(): pl.pallas_call(functools.partial(kernel, nrad, nax), out_shape=tuple((plt...]
where the time goes in v6:
time: 32.4 us; the launch traced here: 32.2 us
  Pallas kernels  31.6 us (98%)
  between operations  0.64 us (2%)
    pallas_call x1, Pallas kernels, local(): pl.pallas_call(functools.partial(kernel, nrad, nax), out_shape=tuple((plt...  29.6 us
    pallas_call x1, Pallas kernels, local(): pl.pallas_call(last_pass, out_shape=(jax.ShapeDtypeStruct(rhs.shape, f32)...  1.94 us

profile of v6, /device:TPU:1, one launch (start us, length us, event | category | flops | bytes accessed | tf_op | source)
XLA Modules:
  0.0 32.2 jit_solution(901802541355885402)
XLA Ops:
  0.6 29.6 %shard_map.95 = (f32[2,2,96,8,128]{4,3,2,1,0:T(8,128)S(1)}, f32[2,2,96,8,128]{4,3,2,1,0:T(8,128)S(1)}, f32[96,8,128]{2,1,0:T(8,128)S(1)}, f32[96,8,128]{2,1,0:T(...) custom-call(f32[2,2,96,8,128]{4,3,2,1,0:T(8,128)} %rhs_hbm.1, ...), custom_call_target="tpu_custom_call" | custom-call | tf_op jit(solution)/shard_map/pallas_call | solution.py:772
  30.3 1.9 %shard_map.96 = (f32[2,2,96,8,128]{4,3,2,1,0:T(8,128)}, f32[2,2,96,8,128]{4,3,2,1,0:T(8,128)}) custom-call(f32[2,2,96,8,128]{4,3,2,1,0:T(8,128)S(1)} %get-tuple-element.13.sol_ref, f32[2,2,96,8,128]{4,3,2,1,0:T(8,128)S(1)} %get-tuple-element.14.val_ref, f32[96,8,128]{2,1,0:T(8,128)S(1)} %get-tuple-element.15.wr_up, ...), custom_call_target="tpu_custom_call" | custom-call | tf_op jit(solution)/shard_map/pallas_call | solution.py:816
